TPU v7x, 32 devices: a whole 2x2x4 slice. The times are simulated.
32 devices in a mesh: groups: 2 (over x), rows: 8 (over z, y), shots: 2 (over core).
Axes of the slice: x: 2, y: 2, z: 4, core: 2. Of those that a mesh axis runs over, the one named last changes fastest.
Arguments:
- right_sides: bfloat16 [2, 16384, 512], P(None, 'rows', ('groups', 'shots')), parts along dimension 2, may hold values from -6 to 6
- panels: bfloat16 [2, 32768, 1024], P(None, ('groups', 'rows')), parts along dimension 1, may hold values from -0.125 to 0.125
- inverses: bfloat16 [8, 2, 256, 256], P('groups'), parts along dimension 0, may hold values from -0.25 to 0.25
- pivots: int32 [4], replicated, may hold values from 0 to 63, as said below
Outputs:
- regrouped: bfloat16 [2, 2, 256, 16384], P(None, 'shots', ('groups', 'rows')), parts along dimension 2
There are 2 independent parts, one for each index of `groups`. A program takes and returns all parts, laid end to end along the dimension named above; an argument that names none is the same for every part. Nothing has to cross between parts.
Inputs may be any that keep to these rules, and one draw needn't show every extreme that they name: `pivots`: 4 distinct row block numbers.
All inputs are finite; a program needn't handle non-finite values.
Results may differ from a plain program's by a relative error of at most 0.0052.
Values may be sent and summed in bfloat16 or wider, within the bound.
No kernel may reach another device: no remote copies, remote signals or barrier semaphores. Data moves between devices by JAX's collectives and lax.ppermute only.
A program may use at most 64 MiB of HBM per device.

v0:
```python
import jax
import jax.numpy as jnp
from jax import lax
from jax.sharding import PartitionSpec as P


def broadcast(block, axis, owner):
    block = jnp.where(lax.axis_index(axis) == owner, block, jnp.zeros_like(block))
    return lax.psum(block, axis)


def complex_dot(matrix, vectors):
    real_part = jnp.dot(matrix[0], vectors[0], preferred_element_type=jnp.float32) - jnp.dot(
        matrix[1], vectors[1], preferred_element_type=jnp.float32
    )
    imag_part = jnp.dot(matrix[0], vectors[1], preferred_element_type=jnp.float32) + jnp.dot(
        matrix[1], vectors[0], preferred_element_type=jnp.float32
    )
    return jnp.stack([real_part, imag_part])


def substitute(running, panels, inverses, pivots, sender):
    my_rank = lax.axis_index("rows")
    local_rows = running.shape[1]
    panel_width = inverses.shape[-1]
    panel_count = inverses.shape[0]
    per_device = local_rows // panel_width
    row_slot = my_rank * per_device + jnp.arange(local_rows, dtype=jnp.int32) // panel_width
    finished = jnp.zeros((local_rows,), dtype=jnp.bool_)
    for panel in range(panel_count):
        pivot_offset = pivots[panel] % per_device * panel_width
        pivot_rows = lax.dynamic_slice_in_dim(running, pivot_offset, panel_width, 1)
        solve_owner_rank = pivots[panel] // per_device

        def on_owner():
            return complex_dot(inverses[panel], pivot_rows.astype(jnp.bfloat16)).astype(
                jnp.bfloat16
            )

        def elsewhere():
            return jnp.zeros(pivot_rows.shape, jnp.bfloat16)

        local_solve = lax.cond(my_rank == solve_owner_rank, on_owner, elsewhere)
        solved = sender(local_solve, solve_owner_rank)
        source = running
        owner_rank = pivots[panel] // per_device
        offset = pivots[panel] % per_device * panel_width
        written = lax.dynamic_update_slice_in_dim(source, solved.astype(jnp.float32), offset, 1)
        source = jnp.where(my_rank == owner_rank, written, source)
        running, finished = (source, finished | (row_slot == pivots[panel]))
        panel_cols = panels[:, :, panel * panel_width : (panel + 1) * panel_width]
        running = jnp.where(
            finished[None, :, None], running, running - complex_dot(panel_cols, solved)
        )
    return running


def body(right_sides, panels, inverses, pivots):
    running = right_sides.astype(jnp.float32)

    def send_whole(local_solve, owner_rank):
        return broadcast(local_solve, "rows", owner_rank)

    running = substitute(running, panels, inverses, pivots, send_whole)
    flipped = jnp.transpose(running, (0, 2, 1)).astype(jnp.bfloat16)
    regrouped = lax.all_to_all(flipped, "rows", split_axis=1, concat_axis=2, tiled=True)
    return regrouped.reshape(2, 1, regrouped.shape[1], regrouped.shape[2])


def solution(mesh):
    placed = (
        P(None, "rows", ("groups", "shots")),
        P(None, ("groups", "rows"), None),
        P("groups", None, None, None),
        P(),
    )
    return jax.shard_map(
        body,
        mesh=mesh,
        in_specs=placed,
        out_specs=P(None, "shots", ("groups", "rows"), None),
        check_vma=False,
    )
```

profile of v0, /device:TPU:0, one launch (start us, length us, event | category | flops | bytes accessed | tf_op | source)
XLA Modules:
  0.0 371.9 jit_solution(8136253707724629650)
XLA Ops:
  10.5 2.3 copy.15
  19.2 68.4 %all-reduce.5.cloned.1.call-done = bf16[2,256,128]{1,2,0:T(8,128)(2,1)} async-done(((bf16[2,256,128]{1,2,0:T(8,128)(2,1)}), bf16[2,256,128]{1,2,0:T(8,128)(2,1)}) %all-reduce.5.cloned.1.call-update) | async-done | bytes 131088 | tf_op jit(solution)/shard_map/psum | solution.py:9
  88.6 1.7 fusion.86
  90.4 1.7 fusion.88
  92.1 1.7 fusion.62
  93.8 1.7 fusion.63
  101.5 65.4 %all-reduce.7.cloned.1.call-done = bf16[2,256,128]{1,2,0:T(8,128)(2,1)} async-done(((bf16[2,256,128]{1,2,0:T(8,128)(2,1)}), bf16[2,256,128]{1,2,0:T(8,128)(2,1)}) %all-reduce.7.cloned.1.call-update) | async-done | bytes 131088 | tf_op jit(solution)/shard_map/psum | solution.py:9
  167.0 1.8 select_dynamic-update-slice_fusion.2
  168.7 1.7 fusion.80
  170.5 1.7 fusion.82
  172.2 1.7 fusion.60
  173.9 1.9 fusion.61
  179.5 1.8 fusion.114
  181.4 65.3 %all-reduce.9.cloned.1.call-done = bf16[2,256,128]{1,2,0:T(8,128)(2,1)} async-done(((bf16[2,256,128]{1,2,0:T(8,128)(2,1)}), bf16[2,256,128]{1,2,0:T(8,128)(2,1)}) %all-reduce.9.cloned.1.call-update) | async-done | bytes 131088 | tf_op jit(solution)/shard_map/psum | solution.py:9
  247.7 2.5 fusion.74
  250.2 1.7 fusion.76
  251.9 1.7 fusion.58
  253.6 1.9 fusion.59
  256.7 2.4 fusion.115
  259.1 67.5 %all-reduce.11.cloned.1.call-done = bf16[2,256,128]{1,2,0:T(8,128)(2,1)} async-done(((bf16[2,256,128]{1,2,0:T(8,128)(2,1)}), bf16[2,256,128]{1,2,0:T(8,128)(2,1)}) %all-reduce.11.cloned.1.call-update) | async-done | bytes 131088 | tf_op jit(solution)/shard_map/psum | solution.py:9
  327.7 1.7 fusion.68
  329.4 1.7 fusion.70
  332.8 1.7 fusion.57
  336.0 27.5 %all_to_all.15 = bf16[2,128,2048]{2,0,1:T(2,128)(2,1)S(1)} all-to-all(bf16[2,128,2048]{2,0,1:T(2,128)(2,1)S(1)} %copy.24), channel_id=1, replica_groups=mesh['groups'=2,'rows'=8,'shots'=2] {'rows'}, dimensions={1} | all-to-all | bytes 2097152 | tf_op jit(solution)/shard_map/all_to_all | solution.py:66
  (63 shorter events, 20.4 us)
Async XLA Ops:
  6.5 81.1 %all-reduce.5.cloned.1.call-start = ((), (), s32[]{:S(2)}) async-start(), calls=%async_computation.1 | async-start | bytes 262144 | tf_op jit(solution)/shard_map/psum | solution.py:9
  12.7 1.6 copy-start.4
  16.1 150.9 %all-reduce.7.cloned.1.call-start = ((), (), s32[]{:S(2)}) async-start(), calls=%async_computation.2 | async-start | bytes 262144 | tf_op jit(solution)/shard_map/psum | solution.py:9
  87.6 2.8 copy-start.6
  95.8 1.3 copy-start.2
  97.9 148.7 %all-reduce.9.cloned.1.call-start = ((), (), s32[]{:S(2)}) async-start(), calls=%async_computation.3 | async-start | bytes 262144 | tf_op jit(solution)/shard_map/psum | solution.py:9
  167.0 3.5 copy-start.7
  173.9 1.9 copy-start.3
  176.9 149.7 %all-reduce.11.cloned.1.call-start = ((), (), s32[]{:S(2)}) async-start(), calls=%async_computation.4 | async-start | bytes 262144 | tf_op jit(solution)/shard_map/psum | solution.py:9
  246.7 3.5 copy-start.5
  247.7 4.2 %copy-start = (f32[2,2048,128]{1,2,0:T(8,128)}, f32[2,2048,128]{1,2,0:T(8,128)S(1)}, u32[]{:S(2)}) copy-start(f32[2,2048,128]{1,2,0:T(8,128)S(1)} %select_dynamic-update-slice_fusion.1) | copy-start | bytes 6291460
  253.6 1.9 copy-start.1
  326.6 2.8 copy-start.8
Sparse Core Ops, SparseCore 0:
  16.2 71.3 all-reduce.4
  98.1 68.8 all-reduce.6
  177.1 69.5 all-reduce.8
  256.8 69.8 all-reduce.10
where the time goes:
time: 373 us; the launch traced here: 372 us
  waiting for transfers between devices  267 us (72%)
  matrix products  29.1 us (8%)
  blocking collectives  27.5 us (7%)
  between operations  23.3 us (6%)
  other arithmetic  16.5 us (4%)
  local copies, waits for them, and re-layouts  8.5 us (2%)
    psum x4, waiting for transfers between devices, broadcast(): return lax.psum(block, axis)  267 us
    all_to_all x1, blocking collectives, body(): lax.all_to_all(flipped, 'rows', split_axis=1, concat_axis=2, tiled=True)  27.5 us
    dot_general x5, matrix products, complex_dot(): jnp.dot(matrix[0], vectors[1], preferred_element_type=jnp.float32)  7.87 us
  transfers between devices with their start and end apart: 4, of which 4 were waited for; matrix products, arithmetic and copies ran while one was open for 2% of the time, Pallas kernels for 0%

commit v1 on v0

v1 whole, which is shorter than its diff:
```python
import functools

import jax
import jax.numpy as jnp
from jax import lax
from jax.experimental import pallas as pl
from jax.experimental.pallas import tpu as pltpu
from jax.sharding import PartitionSpec as P

CONTRACT_LAST = (((1,), (1,)), ((), ()))


def dot_t(left, right):
    return lax.dot_general(left, right, CONTRACT_LAST, preferred_element_type=jnp.float32)


def turned(vectors):
    half = vectors.shape[0] // 2
    return jnp.concatenate([-vectors[half:], vectors[:half]], axis=0)


def transposed_sides(sides):
    shots = sides.shape[2]
    row = lax.broadcasted_iota(jnp.int32, (shots, shots), 0)
    column = lax.broadcasted_iota(jnp.int32, (shots, shots), 1)
    unit = jnp.where(row == column, 1.0, 0.0).astype(jnp.bfloat16)
    return jnp.concatenate([dot_t(unit, sides[0]), dot_t(unit, sides[1])], axis=0)


def solve_kernel(count, slot_ref, sides_ref, inverse_ref, *refs):
    solved_refs, out_ref = refs[:-1], refs[-1]
    rows = transposed_sides(sides_ref)
    width = rows.shape[1]
    if count:
        panel_ref = solved_refs[0]
        for j in range(count):
            solved = solved_refs[1 + j][...]
            columns = slice(j * width, (j + 1) * width)
            rows = rows - dot_t(solved, panel_ref[0, :, columns])
            rows = rows - dot_t(turned(solved), panel_ref[1, :, columns])
    rows = rows.astype(jnp.bfloat16)
    solved = dot_t(rows, inverse_ref[0, 0]) + dot_t(turned(rows), inverse_ref[0, 1])
    out_ref[...] = solved.astype(jnp.bfloat16)


def solve(panel, slot, right_sides, panels, inverses, solved):
    parts, _, shots = right_sides.shape
    width = inverses.shape[-1]
    in_specs = [
        pl.BlockSpec((parts, width, shots), lambda i, s: (0, s[0], 0)),
        pl.BlockSpec((1, parts, width, width), lambda i, s: (panel, 0, 0, 0)),
    ]
    operands = [right_sides, inverses]
    if panel:
        in_specs.append(pl.BlockSpec((parts, width, panel * width), lambda i, s: (0, s[0], 0)))
        operands.append(panels)
    for block in solved:
        in_specs.append(pl.BlockSpec(block.shape, lambda i, s: (0, 0)))
        operands.append(block)
    return pl.pallas_call(
        functools.partial(solve_kernel, panel),
        out_shape=jax.ShapeDtypeStruct((parts * shots, width), jnp.bfloat16),
        grid_spec=pltpu.PrefetchScalarGridSpec(
            num_scalar_prefetch=1,
            grid=(1,),
            in_specs=in_specs,
            out_specs=pl.BlockSpec((parts * shots, width), lambda i, s: (0, 0)),
        ),
        compiler_params=pltpu.CompilerParams(vmem_limit_bytes=32 * 1024 * 1024),
        name="solve",
    )(slot, *operands)


def update_kernel(owners, place_ref, sides_ref, panel_ref, *refs):
    solved_refs, out_ref = refs[:-1], refs[-1]
    width = sides_ref.shape[1]
    block = place_ref[0] + pl.program_id(0)
    rows = transposed_sides(sides_ref)
    for j, solved_ref in enumerate(solved_refs):
        solved = solved_ref[...]
        columns = slice(j * width, (j + 1) * width)
        rows = rows - dot_t(solved, panel_ref[0, :, columns])
        rows = rows - dot_t(turned(solved), panel_ref[1, :, columns])
    shots = rows.shape[0] // 2
    each = shots // owners

    def write(values):
        for part in range(2):
            for owner in range(owners):
                start = part * shots + owner * each
                out_ref[owner, part] = values[start : start + each]

    write(rows.astype(jnp.bfloat16))
    for j, solved_ref in enumerate(solved_refs):

        @pl.when(place_ref[1 + j] == block)
        def _():
            write(solved_ref[...])


def update(place, right_sides, panels, solved, owners):
    parts, local_rows, shots = right_sides.shape
    width = solved[0].shape[1]
    each = shots // owners
    return pl.pallas_call(
        functools.partial(update_kernel, owners),
        out_shape=jax.ShapeDtypeStruct((owners, parts, each, local_rows), jnp.bfloat16),
        grid_spec=pltpu.PrefetchScalarGridSpec(
            num_scalar_prefetch=1,
            grid=(local_rows // width,),
            in_specs=[
                pl.BlockSpec((parts, width, shots), lambda i, s: (0, i, 0)),
                pl.BlockSpec((parts, width, panels.shape[2]), lambda i, s: (0, i, 0)),
            ]
            + [pl.BlockSpec(block.shape, lambda i, s: (0, 0)) for block in solved],
            out_specs=pl.BlockSpec((owners, parts, each, width), lambda i, s: (0, 0, 0, i)),
        ),
        compiler_params=pltpu.CompilerParams(vmem_limit_bytes=32 * 1024 * 1024),
        name="update",
    )(place, right_sides, panels, *solved)


def broadcast_any(block, owner):
    block = jnp.where(lax.axis_index("rows") == owner, block, jnp.zeros_like(block))
    return lax.psum(block, "rows")


def broadcast_pairs(block, owner, ranks):
    me = lax.axis_index("rows")
    lines = ranks // 2

    def branch(source):
        side = source % 2

        def run(value):
            have = jnp.where(me == source, value, jnp.zeros_like(value))
            for line in range(lines):
                if line != source // 2:
                    have = have + lax.ppermute(value, "rows", [(source, line * 2 + side)])
            across = [(line * 2 + side, line * 2 + 1 - side) for line in range(lines)]
            return jnp.where(me % 2 == side, have, lax.ppermute(have, "rows", across))

        return run

    return lax.switch(owner, [branch(source) for source in range(ranks)], block)


def body(ranks, right_sides, panels, inverses, pivots):
    me = lax.axis_index("rows")
    width = inverses.shape[-1]
    per_device = right_sides.shape[1] // width
    solved = []
    for panel in range(inverses.shape[0]):
        owner = pivots[panel] // per_device
        slot = (pivots[panel] % per_device).reshape(1)
        block = solve(panel, slot, right_sides, panels, inverses, solved)
        if ranks % 2 == 0 and ranks <= 8:
            solved.append(broadcast_pairs(block, owner, ranks))
        else:
            solved.append(broadcast_any(block, owner))
    place = jnp.concatenate([(me * per_device).reshape(1), pivots]).astype(jnp.int32)
    rows = update(place, right_sides, panels, solved, ranks)
    received = lax.all_to_all(rows, "rows", split_axis=0, concat_axis=0, tiled=True)
    regrouped = jnp.transpose(received, (1, 2, 0, 3))
    return regrouped.reshape(regrouped.shape[0], 1, regrouped.shape[1], -1)


def solution(mesh):
    placed = (
        P(None, "rows", ("groups", "shots")),
        P(None, ("groups", "rows"), None),
        P("groups", None, None, None),
        P(),
    )
    return jax.shard_map(
        functools.partial(body, mesh.shape["rows"]),
        mesh=mesh,
        in_specs=placed,
        out_specs=P(None, "shots", ("groups", "rows"), None),
        check_vma=False,
    )
```

time: 373 us -> 122 us (0.33)
  waiting for transfers between devices: 267 us -> 40.1 us
  matrix products: 29.1 us -> 0 us
  starting transfers between devices: 0.13 us -> 20.9 us
  other arithmetic: 16.5 us -> 0.92 us
  between operations: 23.3 us -> 10.3 us
  local copies, waits for them, and re-layouts: 8.5 us -> 19.3 us
  Pallas kernels: 0 us -> 8.15 us
  blocking collectives: 27.5 us -> 21.7 us
    psum x4 -> x0, waiting for transfers between devices: 267 us -> none  [broadcast(): return lax.psum(block, axis)]
    ppermute x0 -> x16, waiting for transfers between devices: none -> 40.1 us  [the longest x4 34.4 us: run(): return jnp.where(me % 2 == side, have, lax.ppermute(have, 'rows', across))]
    dot_general x20 -> x0, matrix products: 29.1 us -> none  [the longest x5 7.87 us: complex_dot(): jnp.dot(matrix[0], vectors[1], preferred_element_type=jnp.float32)]
    ppermute x0 -> x16, starting transfers between devices: none -> 20.9 us  [the longest x12 15.7 us: run(): have = have + lax.ppermute(value, 'rows', [(source, line * 2 + side)])]
    unnamed x19 -> x16, local copies, waits for them, and re-layouts: 3.74 us -> 16 us
    select_n x11 -> x4, other arithmetic: 8.48 us -> 0.07 us  [run(): return jnp.where(me % 2 == side, have, lax.ppermute(have, 'rows', across))]
    pallas_call x0 -> x5, Pallas kernels: none -> 8.15 us  [the longest x1 5.76 us: update(): pl.pallas_call(functools.partial(update_kernel, owners), out_shape=jax.Sh...]
    all_to_all x1, blocking collectives: 27.5 us -> 21.7 us  [body(): lax.all_to_all(rows, 'rows', split_axis=0, concat_axis=0, tiled=True)]
  transfers between devices with their start and end apart: 4 -> 16, of which waited for: 4 -> 7; matrix products, arithmetic and copies ran while one was open for 2% -> 0% of each run, Pallas kernels for 0% -> 0%
where the time goes in v1:
time: 122 us
  waiting for transfers between devices  40.1 us (33%)
  blocking collectives  21.7 us (18%)
  starting transfers between devices  20.9 us (17%)
  local copies, waits for them, and re-layouts  19.3 us (16%)
  between operations  10.3 us (8%)
  Pallas kernels  8.15 us (7%)
    ppermute x4, waiting for transfers between devices, run(): return jnp.where(me % 2 == side, have, lax.ppermute(have, 'rows', across))  34.4 us
    all_to_all x1, blocking collectives, body(): lax.all_to_all(rows, 'rows', split_axis=0, concat_axis=0, tiled=True)  21.7 us
    unnamed x16, local copies, waits for them, and re-layouts  16 us
    ppermute x12, starting transfers between devices, run(): have = have + lax.ppermute(value, 'rows', [(source, line * 2 + side)])  15.7 us
    pallas_call x1, Pallas kernels, update(): pl.pallas_call(functools.partial(update_kernel, owners), out_shape=jax.Sh...  5.76 us
    ppermute x12, waiting for transfers between devices, run(): have = have + lax.ppermute(value, 'rows', [(source, line * 2 + side)])  5.75 us
    ppermute x4, starting transfers between devices, run(): return jnp.where(me % 2 == side, have, lax.ppermute(have, 'rows', across))  5.17 us
  transfers between devices with their start and end apart: 16, of which 7 were waited for; matrix products, arithmetic and copies ran while one was open for 0% of the time, Pallas kernels for 0%

profile of v1, /device:TPU:0, one launch (start us, length us, event | category | flops | bytes accessed | tf_op | source)
XLA Modules:
  0.0 122.1 jit_solution(18351513417206118922)
XLA Ops:
  0.0 1.5 %fusion = (s32[1]{0:T(128)}, s32[1]{0:T(128)}, s32[1]{0:T(128)}, s32[1]{0:T(128)}) fusion(s32[4]{0:T(128)} %param.39), kind=kLoop, calls=%fused_computation.65 | loop fusion | bytes 32 | tf_op jit(solution)/shard_map/slice | solution.py:154
  15.2 19.3 %conditional.4 = (bf16[256,256]{1,0:T(8,128)(2,1)S(1)}) conditional(s32[]{:T(128)} %clamp.12, (s32[]{:T(128)}, bf16[256,256]{1,0:T(8,128)(2,1)S(1)}) %tuple.101, (s32[]{:T(128)}, bf16[256,256]{1,0:T(8,128)(2,1)S(1)}) %tuple.101, (s32[]{:T(128)}, bf16[256,256]{1,0:T(8,128)(2,1)S(1)}) %tuple.101, (s32[]{:T(128)}, ...), branch_computations={%region_0.1_spmd, %region_1.2_spmd, %region_2.3_spmd, %region_3.4_... | conditional | flops 327693 | bytes 3146025 | solution.py:145
  15.2 7.1 %collective-permute-start.2 = (bf16[256,256]{1,0:T(8,128)(2,1)S(1)}, bf16[256,256]{1,0:T(8,128)(2,1)S(1)}, u32[]{:S(2)}, u32[]{:S(2)}) collective-permute-start(bf16[256,256]{1,0:T(8,128)(2,1)S(1)} %get-tuple-element.144), channel_id=1, source_target_pairs={{0,12},{1,13},{16,28},{17,29}} | collective-permute-start | bytes 393224 | tf_op jit(solution)/shard_map/cond/branch_0_fun/ppermute | solution.py:139
  22.3 1.3 %collective-permute-start.1 = (bf16[256,256]{1,0:T(8,128)(2,1)S(1)}, bf16[256,256]{1,0:T(8,128)(2,1)S(1)}, u32[]{:S(2)}, u32[]{:S(2)}) collective-permute-start(bf16[256,256]{1,0:T(8,128)(2,1)S(1)} %get-tuple-element.144), channel_id=1, source_target_pairs={{0,8},{1,9},{16,24},{17,25}} | collective-permute-start | bytes 393224 | tf_op jit(solution)/shard_map/cond/branch_0_fun/ppermute | solution.py:139
  23.6 1.3 %collective-permute-start = (bf16[256,256]{1,0:T(8,128)(2,1)S(1)}, bf16[256,256]{1,0:T(8,128)(2,1)S(1)}, u32[]{:S(2)}, u32[]{:S(2)}) collective-permute-start(bf16[256,256]{1,0:T(8,128)(2,1)S(1)} %get-tuple-element.144), channel_id=1, source_target_pairs={{0,4},{1,5},{16,20},{17,21}} | collective-permute-start | bytes 393224 | tf_op jit(solution)/shard_map/cond/branch_0_fun/ppermute | solution.py:139
  26.2 2.8 %collective-permute-done.1 = bf16[256,256]{1,0:T(8,128)(2,1)S(1)} collective-permute-done((bf16[256,256]{1,0:T(8,128)(2,1)S(1)}, bf16[256,256]{1,0:T(8,128)(2,1)S(1)}, u32[]{:S(2)}, u32[]{:S(2)}) %collective-permute-start.1) | collective-permute-done | bytes 131104 | tf_op jit(solution)/shard_map/cond/branch_0_fun/ppermute | solution.py:139
  29.0 1.7 %collective-permute-done = bf16[256,256]{1,0:T(8,128)(2,1)S(1)} collective-permute-done((bf16[256,256]{1,0:T(8,128)(2,1)S(1)}, bf16[256,256]{1,0:T(8,128)(2,1)S(1)}, u32[]{:S(2)}, u32[]{:S(2)}) %collective-permute-start) | collective-permute-done | bytes 131104 | tf_op jit(solution)/shard_map/cond/branch_0_fun/ppermute | solution.py:139
  30.7 1.3 %collective-permute-start.3 = (bf16[256,256]{1,0:T(8,128)(2,1)S(1)}, bf16[256,256]{1,0:T(8,128)(2,1)S(1)}, u32[]{:S(2)}, u32[]{:S(2)}) collective-permute-start(bf16[256,256]{1,0:T(8,128)(2,1)S(1)} %add_add_fusion), channel_id=1, source_target_pairs={{0,2},{4,6},{8,10},{12,14},{1,3},{5,7},{9,11},{13,15},{16,18},{20,... | collective-permute-start | bytes 393224 | tf_op jit(solution)/shard_map/cond/branch_0_fun/ppermute | solution.py:141
  32.0 2.5 %collective-permute-done.3 = bf16[256,256]{1,0:T(8,128)(2,1)S(1)} collective-permute-done((bf16[256,256]{1,0:T(8,128)(2,1)S(1)}, bf16[256,256]{1,0:T(8,128)(2,1)S(1)}, u32[]{:S(2)}, u32[]{:S(2)}) %collective-permute-start.3) | collective-permute-done | bytes 131104 | tf_op jit(solution)/shard_map/cond/branch_0_fun/ppermute | solution.py:141
  34.5 3.4 %copy-done = bf16[2,2048,1024]{2,1,0:T(8,128)(2,1)S(1)} copy-done((bf16[2,2048,1024]{2,1,0:T(8,128)(2,1)S(1)}, bf16[2,2048,1024]{2,1,0:T(8,128)(2,1)}, u32[]{:S(2)}) %copy-start) | copy-done | bytes 8388632
  38.5 15.2 %conditional.5 = (bf16[256,256]{1,0:T(8,128)(2,1)S(1)}) conditional(s32[]{:T(128)} %clamp.13, (s32[]{:T(128)}, bf16[256,256]{1,0:T(8,128)(2,1)S(1)}) %tuple.102, (s32[]{:T(128)}, bf16[256,256]{1,0:T(8,128)(2,1)S(1)}) %tuple.102, (s32[]{:T(128)}, bf16[256,256]{1,0:T(8,128)(2,1)S(1)}) %tuple.102, (s32[]{:T(128)}, ...), branch_computations={%region_8.9_spmd, %region_9.10_spmd, %region_10.11_spmd, %region_1... | conditional | flops 327693 | bytes 3146025 | solution.py:145
  40.7 1.3 %collective-permute-start.39 = (bf16[256,256]{1,0:T(8,128)(2,1)S(1)}, bf16[256,256]{1,0:T(8,128)(2,1)S(1)}, u32[]{:S(2)}, u32[]{:S(2)}) collective-permute-start(bf16[256,256]{1,0:T(8,128)(2,1)S(1)} %add_add_fusion.9), channel_id=1, source_target_pairs={{2,0},{6,4},{10,8},{14,12},{3,1},{7,5},{11,9},{15,13},{18,16},{22,... | collective-permute-start | bytes 393224 | tf_op jit(solution)/shard_map/cond/branch_1_fun/ppermute | solution.py:141
  42.0 11.7 %collective-permute-done.39 = bf16[256,256]{1,0:T(8,128)(2,1)S(1)} collective-permute-done((bf16[256,256]{1,0:T(8,128)(2,1)S(1)}, bf16[256,256]{1,0:T(8,128)(2,1)S(1)}, u32[]{:S(2)}, u32[]{:S(2)}) %collective-permute-start.39) | collective-permute-done | bytes 131104 | tf_op jit(solution)/shard_map/cond/branch_1_fun/ppermute | solution.py:141
  53.7 3.4 %copy-done.1 = bf16[2,2048,1024]{2,1,0:T(8,128)(2,1)S(1)} copy-done((bf16[2,2048,1024]{2,1,0:T(8,128)(2,1)S(1)}, bf16[2,2048,1024]{2,1,0:T(8,128)(2,1)}, u32[]{:S(2)}) %copy-start.1) | copy-done | bytes 8388632
  57.8 13.3 %conditional.6 = (bf16[256,256]{1,0:T(8,128)(2,1)S(1)}) conditional(s32[]{:T(128)} %clamp.14, (s32[]{:T(128)}, bf16[256,256]{1,0:T(8,128)(2,1)S(1)}) %tuple.103, (s32[]{:T(128)}, bf16[256,256]{1,0:T(8,128)(2,1)S(1)}) %tuple.103, (s32[]{:T(128)}, bf16[256,256]{1,0:T(8,128)(2,1)S(1)}) %tuple.103, (s32[]{:T(128)}, ...), branch_computations={%region_16.17_spmd, %region_17.18_spmd, %region_18.19_spmd, %regio... | conditional | flops 327693 | bytes 3146025 | solution.py:145
  61.2 9.8 %collective-permute-done.79 = bf16[256,256]{1,0:T(8,128)(2,1)S(1)} collective-permute-done((bf16[256,256]{1,0:T(8,128)(2,1)S(1)}, bf16[256,256]{1,0:T(8,128)(2,1)S(1)}, u32[]{:S(2)}, u32[]{:S(2)}) %collective-permute-start.79) | collective-permute-done | bytes 131104 | tf_op jit(solution)/shard_map/cond/branch_3_fun/ppermute | solution.py:141
  71.1 3.4 %copy-done.2 = bf16[2,2048,1024]{2,1,0:T(8,128)(2,1)S(1)} copy-done((bf16[2,2048,1024]{2,1,0:T(8,128)(2,1)S(1)}, bf16[2,2048,1024]{2,1,0:T(8,128)(2,1)}, u32[]{:S(2)}) %copy-start.2) | copy-done | bytes 8388632
  75.2 14.1 %conditional.7 = (bf16[256,256]{1,0:T(8,128)(2,1)S(1)}) conditional(s32[]{:T(128)} %clamp.15, (s32[]{:T(128)}, bf16[256,256]{1,0:T(8,128)(2,1)S(1)}) %tuple.104, (s32[]{:T(128)}, bf16[256,256]{1,0:T(8,128)(2,1)S(1)}) %tuple.104, (s32[]{:T(128)}, bf16[256,256]{1,0:T(8,128)(2,1)S(1)}) %tuple.104, (s32[]{:T(128)}, ...), branch_computations={%region_24.25_spmd, %region_25.26_spmd, %region_26.27_spmd, %regio... | conditional | flops 327693 | bytes 3146025 | solution.py:145
  77.5 1.3 %collective-permute-start.127 = (bf16[256,256]{1,0:T(8,128)(2,1)S(1)}, bf16[256,256]{1,0:T(8,128)(2,1)S(1)}, u32[]{:S(2)}, u32[]{:S(2)}) collective-permute-start(bf16[256,256]{1,0:T(8,128)(2,1)S(1)} %add_add_fusion.31), channel_id=1, source_target_pairs={{2,0},{6,4},{10,8},{14,12},{3,1},{7,5},{11,9},{15,13},{18,16},{22,... | collective-permute-start | bytes 393224 | tf_op jit(solution)/shard_map/cond/branch_7_fun/ppermute | solution.py:141
  78.8 10.4 %collective-permute-done.127 = bf16[256,256]{1,0:T(8,128)(2,1)S(1)} collective-permute-done((bf16[256,256]{1,0:T(8,128)(2,1)S(1)}, bf16[256,256]{1,0:T(8,128)(2,1)S(1)}, u32[]{:S(2)}, u32[]{:S(2)}) %collective-permute-start.127) | collective-permute-done | bytes 131104 | tf_op jit(solution)/shard_map/cond/branch_7_fun/ppermute | solution.py:141
  89.3 3.4 %copy-done.3 = bf16[2,2048,1024]{2,1,0:T(8,128)(2,1)S(1)} copy-done((bf16[2,2048,1024]{2,1,0:T(8,128)(2,1)S(1)}, bf16[2,2048,1024]{2,1,0:T(8,128)(2,1)}, u32[]{:S(2)}) %copy-start.3) | copy-done | bytes 8388632
  92.7 5.8 %update.1 = bf16[8,2,16,2048]{3,2,1,0:T(8,128)(2,1)S(1)} custom-call(s32[5]{0:T(128)S(1)} %pad_add_fusion.place_ref, bf16[2,2048,128]{2,1,0:T(8,128)(2,1)S(1)} %copy-done.5, bf16[2,2048,1024]{2,1,0:T(8,128)(2,1)S(1)} %copy-done.3, bf16[256,256]{1,0:T(8,128)(2,1)S(1)} %get-tuple-element.237.refs_1_.refs_0_, ...), custom_call_target="tpu_custom_call" | custom-call | tf_op jit(solution)/shard_map/update/pallas_call | solution.py:105
  98.4 21.7 %all_to_all.5 = bf16[8,2,16,2048]{3,2,1,0:T(8,128)(2,1)S(1)} all-to-all(bf16[8,2,16,2048]{3,2,1,0:T(8,128)(2,1)S(1)} %update.1), channel_id=1, replica_groups=mesh['groups'=2,'rows'=8,'shots'=2] {'rows'}, dimensions={0} | all-to-all | bytes 2097152 | tf_op jit(solution)/shard_map/all_to_all | solution.py:163
  120.7 1.3 %reshape.23 = bf16[2,1,16,16384]{3,2,0,1:T(8,128)(2,1)} reshape(bf16[2,16,8,2048]{3,2,1,0:T(8,128)(2,1)S(1)} %copy.5) | data formatting | bytes 2097152 | tf_op jit(solution)/shard_map/reshape | solution.py:165
  (46 shorter events, 15.0 us)
Async XLA Ops:
  12.3 1.2 %copy-start.4 = (bf16[2,2048,128]{2,1,0:T(8,128)(2,1)S(1)}, bf16[2,2048,128]{2,1,0:T(8,128)(2,1)}, u32[]{:S(2)}) copy-start(bf16[2,2048,128]{2,1,0:T(8,128)(2,1)} %sides_ref.9) | copy-start | bytes 3145732
  13.6 1.2 %copy-start.6 = (bf16[4,2,256,256]{3,2,1,0:T(8,128)(2,1)S(1)}, bf16[4,2,256,256]{3,2,1,0:T(8,128)(2,1)}, u32[]{:S(2)}) copy-start(bf16[4,2,256,256]{3,2,1,0:T(8,128)(2,1)} %inverse_ref.7) | copy-start | bytes 3145732
  14.8 19.7 %copy-start.5 = (bf16[2,2048,128]{2,1,0:T(8,128)(2,1)S(1)}, bf16[2,2048,128]{2,1,0:T(8,128)(2,1)}, u32[]{:S(2)}) copy-start(bf16[2,2048,128]{2,1,0:T(8,128)(2,1)} %sides_ref.9) | copy-start | bytes 3145732
  14.8 19.7 %copy-start.7 = (bf16[4,2,256,256]{3,2,1,0:T(8,128)(2,1)S(1)}, bf16[4,2,256,256]{3,2,1,0:T(8,128)(2,1)}, u32[]{:S(2)}) copy-start(bf16[4,2,256,256]{3,2,1,0:T(8,128)(2,1)} %inverse_ref.7) | copy-start | bytes 3145732
  15.2 11.0 %collective-permute-start.2 = (bf16[256,256]{1,0:T(8,128)(2,1)S(1)}, bf16[256,256]{1,0:T(8,128)(2,1)S(1)}, u32[]{:S(2)}, u32[]{:S(2)}) collective-permute-start(bf16[256,256]{1,0:T(8,128)(2,1)S(1)} %get-tuple-element.144), channel_id=1, source_target_pairs={{0,12},{1,13},{16,28},{17,29}} | collective-permute-start | bytes 393224 | tf_op jit(solution)/shard_map/cond/branch_0_fun/ppermute | solution.py:139
  22.3 6.7 %collective-permute-start.1 = (bf16[256,256]{1,0:T(8,128)(2,1)S(1)}, bf16[256,256]{1,0:T(8,128)(2,1)S(1)}, u32[]{:S(2)}, u32[]{:S(2)}) collective-permute-start(bf16[256,256]{1,0:T(8,128)(2,1)S(1)} %get-tuple-element.144), channel_id=1, source_target_pairs={{0,8},{1,9},{16,24},{17,25}} | collective-permute-start | bytes 393224 | tf_op jit(solution)/shard_map/cond/branch_0_fun/ppermute | solution.py:139
  23.6 7.0 %collective-permute-start = (bf16[256,256]{1,0:T(8,128)(2,1)S(1)}, bf16[256,256]{1,0:T(8,128)(2,1)S(1)}, u32[]{:S(2)}, u32[]{:S(2)}) collective-permute-start(bf16[256,256]{1,0:T(8,128)(2,1)S(1)} %get-tuple-element.144), channel_id=1, source_target_pairs={{0,4},{1,5},{16,20},{17,21}} | collective-permute-start | bytes 393224 | tf_op jit(solution)/shard_map/cond/branch_0_fun/ppermute | solution.py:139
  30.7 3.8 %collective-permute-start.3 = (bf16[256,256]{1,0:T(8,128)(2,1)S(1)}, bf16[256,256]{1,0:T(8,128)(2,1)S(1)}, u32[]{:S(2)}, u32[]{:S(2)}) collective-permute-start(bf16[256,256]{1,0:T(8,128)(2,1)S(1)} %add_add_fusion), channel_id=1, source_target_pairs={{0,2},{4,6},{8,10},{12,14},{1,3},{5,7},{9,11},{13,15},{16,18},{20,... | collective-permute-start | bytes 393224 | tf_op jit(solution)/shard_map/cond/branch_0_fun/ppermute | solution.py:141
  34.5 3.4 %copy-start = (bf16[2,2048,1024]{2,1,0:T(8,128)(2,1)S(1)}, bf16[2,2048,1024]{2,1,0:T(8,128)(2,1)}, u32[]{:S(2)}) copy-start(bf16[2,2048,1024]{2,1,0:T(8,128)(2,1)} %panel_ref.1) | copy-start | bytes 25165828
  38.5 2.0 %collective-permute-start.38 = (bf16[256,256]{1,0:T(8,128)(2,1)S(1)}, bf16[256,256]{1,0:T(8,128)(2,1)S(1)}, u32[]{:S(2)}, u32[]{:S(2)}) collective-permute-start(bf16[256,256]{1,0:T(8,128)(2,1)S(1)} %get-tuple-element.180), channel_id=1, source_target_pairs={{2,14},{3,15},{18,30},{19,31}} | collective-permute-start | bytes 393224 | tf_op jit(solution)/shard_map/cond/branch_1_fun/ppermute | solution.py:139
  39.2 1.4 %collective-permute-start.37 = (bf16[256,256]{1,0:T(8,128)(2,1)S(1)}, bf16[256,256]{1,0:T(8,128)(2,1)S(1)}, u32[]{:S(2)}, u32[]{:S(2)}) collective-permute-start(bf16[256,256]{1,0:T(8,128)(2,1)S(1)} %get-tuple-element.180), channel_id=1, source_target_pairs={{2,10},{3,11},{18,26},{19,27}} | collective-permute-start | bytes 393224 | tf_op jit(solution)/shard_map/cond/branch_1_fun/ppermute | solution.py:139
  39.9 0.7 collective-permute-start.36
  40.7 13.0 %collective-permute-start.39 = (bf16[256,256]{1,0:T(8,128)(2,1)S(1)}, bf16[256,256]{1,0:T(8,128)(2,1)S(1)}, u32[]{:S(2)}, u32[]{:S(2)}) collective-permute-start(bf16[256,256]{1,0:T(8,128)(2,1)S(1)} %add_add_fusion.9), channel_id=1, source_target_pairs={{2,0},{6,4},{10,8},{14,12},{3,1},{7,5},{11,9},{15,13},{18,16},{22,... | collective-permute-start | bytes 393224 | tf_op jit(solution)/shard_map/cond/branch_1_fun/ppermute | solution.py:141
  53.7 3.4 %copy-start.1 = (bf16[2,2048,1024]{2,1,0:T(8,128)(2,1)S(1)}, bf16[2,2048,1024]{2,1,0:T(8,128)(2,1)}, u32[]{:S(2)}) copy-start(bf16[2,2048,1024]{2,1,0:T(8,128)(2,1)} %panel_ref.1) | copy-start | bytes 25165828
  57.8 2.0 %collective-permute-start.78 = (bf16[256,256]{1,0:T(8,128)(2,1)S(1)}, bf16[256,256]{1,0:T(8,128)(2,1)S(1)}, u32[]{:S(2)}, u32[]{:S(2)}) collective-permute-start(bf16[256,256]{1,0:T(8,128)(2,1)S(1)} %get-tuple-element.208), channel_id=1, source_target_pairs={{6,14},{7,15},{22,30},{23,31}} | collective-permute-start | bytes 393224 | tf_op jit(solution)/shard_map/cond/branch_3_fun/ppermute | solution.py:139
  58.5 1.4 %collective-permute-start.77 = (bf16[256,256]{1,0:T(8,128)(2,1)S(1)}, bf16[256,256]{1,0:T(8,128)(2,1)S(1)}, u32[]{:S(2)}, u32[]{:S(2)}) collective-permute-start(bf16[256,256]{1,0:T(8,128)(2,1)S(1)} %get-tuple-element.208), channel_id=1, source_target_pairs={{6,10},{7,11},{22,26},{23,27}} | collective-permute-start | bytes 393224 | tf_op jit(solution)/shard_map/cond/branch_3_fun/ppermute | solution.py:139
  59.2 0.7 collective-permute-start.76
  59.9 11.1 %collective-permute-start.79 = (bf16[256,256]{1,0:T(8,128)(2,1)S(1)}, bf16[256,256]{1,0:T(8,128)(2,1)S(1)}, u32[]{:S(2)}, u32[]{:S(2)}) collective-permute-start(bf16[256,256]{1,0:T(8,128)(2,1)S(1)} %add_add_fusion.19), channel_id=1, source_target_pairs={{2,0},{6,4},{10,8},{14,12},{3,1},{7,5},{11,9},{15,13},{18,16},{22,... | collective-permute-start | bytes 393224 | tf_op jit(solution)/shard_map/cond/branch_3_fun/ppermute | solution.py:141
  71.0 3.4 %copy-start.2 = (bf16[2,2048,1024]{2,1,0:T(8,128)(2,1)S(1)}, bf16[2,2048,1024]{2,1,0:T(8,128)(2,1)}, u32[]{:S(2)}) copy-start(bf16[2,2048,1024]{2,1,0:T(8,128)(2,1)} %panel_ref.1) | copy-start | bytes 25165828
  75.4 2.0 %collective-permute-start.126 = (bf16[256,256]{1,0:T(8,128)(2,1)S(1)}, bf16[256,256]{1,0:T(8,128)(2,1)S(1)}, u32[]{:S(2)}, u32[]{:S(2)}) collective-permute-start(bf16[256,256]{1,0:T(8,128)(2,1)S(1)} %get-tuple-element.232), channel_id=1, source_target_pairs={{14,10},{15,11},{30,26},{31,27}} | collective-permute-start | bytes 393224 | tf_op jit(solution)/shard_map/cond/branch_7_fun/ppermute | solution.py:139
  76.1 1.4 %collective-permute-start.125 = (bf16[256,256]{1,0:T(8,128)(2,1)S(1)}, bf16[256,256]{1,0:T(8,128)(2,1)S(1)}, u32[]{:S(2)}, u32[]{:S(2)}) collective-permute-start(bf16[256,256]{1,0:T(8,128)(2,1)S(1)} %get-tuple-element.232), channel_id=1, source_target_pairs={{14,6},{15,7},{30,22},{31,23}} | collective-permute-start | bytes 393224 | tf_op jit(solution)/shard_map/cond/branch_7_fun/ppermute | solution.py:139
  76.8 0.7 collective-permute-start.124
  77.5 11.7 %collective-permute-start.127 = (bf16[256,256]{1,0:T(8,128)(2,1)S(1)}, bf16[256,256]{1,0:T(8,128)(2,1)S(1)}, u32[]{:S(2)}, u32[]{:S(2)}) collective-permute-start(bf16[256,256]{1,0:T(8,128)(2,1)S(1)} %add_add_fusion.31), channel_id=1, source_target_pairs={{2,0},{6,4},{10,8},{14,12},{3,1},{7,5},{11,9},{15,13},{18,16},{22,... | collective-permute-start | bytes 393224 | tf_op jit(solution)/shard_map/cond/branch_7_fun/ppermute | solution.py:141
  89.3 3.4 %copy-start.3 = (bf16[2,2048,1024]{2,1,0:T(8,128)(2,1)S(1)}, bf16[2,2048,1024]{2,1,0:T(8,128)(2,1)}, u32[]{:S(2)}) copy-start(bf16[2,2048,1024]{2,1,0:T(8,128)(2,1)} %panel_ref.1) | copy-start | bytes 25165828
